TPU v7x, 512 devices: a whole 4x8x8 slice. The times are simulated.
512 devices in a mesh: grp: 32 (over z, y_lo, core), row: 16 (over y_hi, x).
Axes of the slice: x: 4, y: 8 (y_hi: 4, y_lo: 2; y = y_hi * 2 + y_lo), z: 8, core: 2. Of those that a mesh axis runs over, the one named last changes fastest.
Arguments:
- amplitudes: bfloat16 [512, 1792], P(('grp', 'row')), may hold values from -6 to 6
- integrals: bfloat16 [1792, 524288], P(None, ('grp', 'row')), may hold values from -0.125 to 0.125
- occ_energy: float32 [512], replicated, may hold values from -3 to -1
- virt_energy: float32 [524288], P('grp'), may hold values from 1 to 4
Outputs:
- new_amplitudes: bfloat16 [512, 524288], P('row', 'grp')
All inputs are finite; a program needn't handle non-finite values.
Results may differ from a plain program's by a relative error of at most 0.001.
Values may be sent and summed in bfloat16 or wider, within the bound.
No kernel may reach another device: no remote copies, remote signals or barrier semaphores. Data moves between devices by JAX's collectives and lax.ppermute only.
A program may use at most 64 MiB of HBM per device.

v0:
```python
import jax
import jax.numpy as jnp
from jax import lax
from jax.sharding import PartitionSpec as P


def shards(amplitudes, integrals, occ_energy, virt_energy):
    ladder = jnp.dot(
        lax.all_gather(amplitudes, ("grp", "row"), axis=0, tiled=True),
        integrals,
        preferred_element_type=jnp.float32,
    )
    row_index = lax.axis_index("row")
    received = lax.all_to_all(ladder, "row", split_axis=0, concat_axis=1, tiled=True)
    block_rows = received.shape[0]
    occ_rows = lax.dynamic_slice_in_dim(occ_energy, row_index * block_rows, block_rows, 0)
    result = (received / (virt_energy[None, :] - occ_rows[:, None])).astype(jnp.bfloat16)
    return result


def solution(mesh):
    return jax.shard_map(
        shards,
        mesh=mesh,
        in_specs=(P(("grp", "row"), None), P(None, ("grp", "row")), P(), P("grp")),
        out_specs=P("row", "grp"),
        check_vma=False,
    )
```

profile of v0, /device:TPU:1, one launch (start us, length us, event | category | flops | bytes accessed | tf_op | source)
XLA Modules:
  0.0 1464.8 jit_solution(7006868943935501536)
XLA Ops:
  6.5 0.0 all-gather.3.cloned.1.call-start
  6.5 0.7 all-gather.3.cloned.1.call-update
  7.3 1388.2 %all-gather.3.cloned.1.call-done = bf16[512,1,1792]{2,1,0:T(2,128)(2,1)} async-done(((bf16[1,1,1792]{2,1,0:T(2,128)(2,1)}), bf16[512,1,1792]{2,1,0:T(2,128)(2,1)}) %all-gather.3.cloned.1.call-update) | async-done | bytes 1835024 | tf_op jit(solution)/shard_map/all_gather | solution.py:9
  1395.4 6.6 fusion
  1402.0 10.1 all-to-all-start
  1412.1 0.8 dynamic_slice.3
  1412.8 43.0 %all-to-all-done = f32[16,32,1024]{2,1,0:T(8,128)S(1)} async-done(((f32[16,32,1024]{2,1,0:T(8,128)}), f32[16,32,1024]{2,1,0:T(8,128)S(1)}, u32[]{:S(2)}, u32[]{:S(2)}) %all-to-all-start) | async-done | bytes 2097184 | tf_op jit(solution)/shard_map/all_to_all | solution.py:14
  1455.8 0.0 copy-start
  1455.8 0.2 copy.9
  1456.1 0.6 copy-done
  1456.7 1.3 divide_convert_fusion
Async XLA Ops:
  6.5 1388.9 %all-gather.3.cloned.1.call-start = ((), (), s32[]{:S(2)}) async-start(), calls=%async_computation.1 | async-start | bytes 3677184 | tf_op jit(solution)/shard_map/all_gather | solution.py:9
  1402.0 53.8 %all-to-all-start = ((f32[16,32,1024]{2,1,0:T(8,128)}), f32[16,32,1024]{2,1,0:T(8,128)S(1)}, u32[]{:S(2)}, u32[]{:S(2)}) async-start(f32[16,32,1024]{2,1,0:T(8,128)} %bitcast.11), calls=%async_computation | async-start | bytes 4194304 | tf_op jit(solution)/shard_map/all_to_all | solution.py:14
  1455.8 0.8 copy-start
Sparse Core Ops, SparseCore 0:
  9.6 1385.7 all-gather.2
where the time goes:
time: 1480 us; the launch traced here: 1460 us
  waiting for transfers between devices  1430 us (97%)
    all_gather x1, waiting for transfers between devices, shards(): lax.all_gather(amplitudes, ('grp', 'row'), axis=0, tiled=True)  1390 us
    all_to_all x1, waiting for transfers between devices, shards(): lax.all_to_all(ladder, 'row', split_axis=0, concat_axis=1, tiled=True)  43 us
  transfers between devices with their start and end apart: 2, of which 2 were waited for; matrix products, arithmetic and copies ran while one was open for 0% of the time, Pallas kernels for 0%

commit v1 on v0

v1 whole, which is shorter than its diff:
```python
import jax
import jax.numpy as jnp
from jax import lax
from jax.sharding import Mesh, PartitionSpec as P

FINE = ("z", "yl", "c", "yh", "x")
SIZES = (8, 2, 2, 4, 4)


def spread(value, axes, peers):
    copies = jnp.broadcast_to(value[None], (peers,) + value.shape)
    return lax.all_to_all(copies, axes, split_axis=0, concat_axis=0, tiled=True)


def shards(amplitudes, integrals, occ_energy, virt_energy):
    row = amplitudes.reshape(14, 128)
    plane = spread(row, ("z", "yl", "yh"), 64)
    half = spread(plane, ("x",), 4)
    half = half.reshape(4, 16, 4, 14, 128).transpose(1, 2, 0, 3, 4).reshape(256, 1792)
    other = lax.ppermute(half, "c", [(0, 1), (1, 0)])

    core = lax.axis_index("c")
    member = lax.axis_index(("yh", "x"))
    virt = lax.dynamic_slice_in_dim(virt_energy, member * 1024, 1024, 0)
    occ = occ_energy.reshape(16, 2, 16)

    def update(rows, which):
        ladder = jnp.dot(rows, integrals, preferred_element_type=jnp.float32)
        occ_rows = lax.dynamic_index_in_dim(occ, which, 1, keepdims=False)
        gap = virt[None, None, :] - occ_rows[:, :, None]
        return (ladder.reshape(16, 16, 1024) / gap).astype(jnp.bfloat16)

    pair = jnp.stack([update(half, core), update(other, 1 - core)], axis=1)
    got = lax.all_to_all(
        pair, ("yh", "x"), split_axis=0, concat_axis=0, tiled=True
    )
    first = jnp.where(core == 0, got[:, 0], got[:, 1])
    second = jnp.where(core == 0, got[:, 1], got[:, 0])
    result = jnp.stack([first, second], axis=0)
    return result.transpose(0, 2, 1, 3).reshape(32, 16384)


def solution(mesh):
    fine = Mesh(mesh.devices.reshape(SIZES), FINE)
    return jax.shard_map(
        shards,
        mesh=fine,
        in_specs=(
            P(FINE, None),
            P(None, FINE),
            P(),
            P(("z", "yl", "c")),
        ),
        out_specs=P(("yh", "x"), ("z", "yl", "c")),
        check_vma=False,
    )
```

time: 1480 us -> 96.8 us (0.07); the launches traced: 1460 us -> 96.4 us
  waiting for transfers between devices: 1430 us -> 28.9 us
  blocking collectives: 0 us -> 45 us
    all_gather x1 -> x0, waiting for transfers between devices: 1390 us -> none  [shards(): lax.all_gather(amplitudes, ('grp', 'row'), axis=0, tiled=True)]
    all_to_all x0 -> x2, blocking collectives: none -> 45 us  [spread(): return lax.all_to_all(copies, axes, split_axis=0, concat_axis=0, tiled=True)]
  transfers between devices with their start and end apart: 2 -> 2, of which waited for: 2 -> 1; matrix products, arithmetic and copies ran while one was open for 0% -> 5% of each run, Pallas kernels for 0% -> 0%
where the time goes in v1:
time: 96.8 us; the launch traced here: 96.4 us
  blocking collectives  45 us (46%)
  waiting for transfers between devices  28.9 us (30%)
  starting transfers between devices  9.57 us (10%)
  local copies, waits for them, and re-layouts  5.81 us (6%)
  matrix products  5.67 us (6%)
  other arithmetic  1.25 us (1%)
    all_to_all x2, blocking collectives, spread(): return lax.all_to_all(copies, axes, split_axis=0, concat_axis=0, tiled=True)  45 us
    all_to_all x1, waiting for transfers between devices, shards(): lax.all_to_all(pair, ('yh', 'x'), split_axis=0, concat_axis=0, tiled=True)  28.9 us
    ppermute x1, starting transfers between devices, shards(): other = lax.ppermute(half, 'c', [(0, 1), (1, 0)])  5.85 us
    dot_general x2, matrix products, update(): ladder = jnp.dot(rows, integrals, preferred_element_type=jnp.float32)  5.67 us
    all_to_all x1, starting transfers between devices, shards(): lax.all_to_all(pair, ('yh', 'x'), split_axis=0, concat_axis=0, tiled=True)  3.72 us
  transfers between devices with their start and end apart: 2, of which 1 were waited for; matrix products, arithmetic and copies ran while one was open for 5% of the time, Pallas kernels for 0%

profile of v1, /device:TPU:1, one launch (start us, length us, event | category | flops | bytes accessed | tf_op | source)
XLA Modules:
  0.0 96.4 jit_solution(5652252453744451412)
XLA Ops:
  0.0 0.7 reduce
  0.8 30.5 %all_to_all.15 = bf16[64,14,128]{2,1,0:T(8,128)(2,1)S(1)} all-to-all(bf16[64,14,128]{2,1,0:T(8,128)(2,1)S(1)} %broadcast_in_dim.7), channel_id=1, replica_groups=mesh['z'=8,'yl'=2,'c'=2,'yh'=4,'x'=4] {'z','yl','yh'}, dimensions={0} | all-to-all | bytes 458752 | tf_op jit(solution)/shard_map/all_to_all | solution.py:12
  31.3 0.0 copy-start
  31.3 0.1 copy.13
  31.4 0.2 broadcast_in_dim.8
  31.6 14.5 %all_to_all.16 = bf16[4,64,14,128]{3,1,2,0:T(8,128)(2,1)S(1)} all-to-all(bf16[4,64,14,128]{3,1,2,0:T(8,128)(2,1)S(1)} %broadcast_in_dim.8), channel_id=1, replica_groups=mesh['z'=8,'yl'=2,'c'=2,'yh'=4,'x'=4] {'x'}, dimensions={0} | all-to-all | bytes 1835008 | tf_op jit(solution)/shard_map/all_to_all | solution.py:12
  46.1 0.6 copy.28
  46.7 0.2 copy.27
  47.0 5.8 %collective-permute-start = (bf16[256,1792]{1,0:T(8,128)(2,1)S(1)}, bf16[256,1792]{1,0:T(8,128)(2,1)}, u32[]{:S(2)}, u32[]{:S(2)}) collective-permute-start(bf16[256,1792]{1,0:T(8,128)(2,1)S(1)} %bitcast.53), channel_id=1, source_target_pairs={{0,16},{16,0},{1,17},{17,1},{2,18},{18,2},{3,19},{19,3},{4,20},{20... | collective-permute-start | bytes 2752520 | tf_op jit(solution)/shard_map/ppermute | solution.py:20
  52.8 0.0 copy-done
  52.8 0.1 reshape.80
  52.9 0.7 dynamic_slice.10
  53.6 0.7 dot_general.8
  54.3 0.0 copy-start.1
  54.3 3.4 %fusion.8 = bf16[16,1,16,1024]{3,2,0,1:T(8,128)(2,1)S(1)} fusion(bf16[16,16,1792]{2,1,0:T(8,128)(2,1)S(1)} %dot_general.8, bf16[1792,1024]{1,0:T(8,128)(2,1)} %param.5, f32[16,16]{1,0:T(8,128)S(1)} %bitcast.56, f32[1024]{0:T(1024)S(1)} %dynamic_slice.10), kind=kOutput, calls=%fused_computation.4 | convolution fusion | flops 940310528 | bytes 5116928 | tf_op jit(solution)/shard_map/dot_general | solution.py:28
  57.7 0.0 collective-permute-done
  57.7 0.0 copy-done.1
  57.7 2.3 %fusion.13 = f32[256,1024]{1,0:T(8,128)S(1)} fusion(bf16[256,1792]{1,0:T(8,128)(2,1)} %collective-permute-done, bf16[1792,1024]{1,0:T(8,128)(2,1)S(1)} %copy-done.1), kind=kOutput, calls=%fused_computation.16 | convolution fusion | flops 939524096 | bytes 5636096 | tf_op jit(solution)/shard_map/dot_general | solution.py:28
  60.0 0.2 divide_convert_fusion
  60.2 0.1 pad_maximum_fusion
  60.3 1.0 %copy.15 = bf16[16,2,16,1024]{3,2,1,0:T(8,128)(2,1)} copy(bf16[16,2,16,1024]{3,2,0,1:T(8,128)(2,1)S(1)} %pad_maximum_fusion) | data formatting | bytes 2097152 | tf_op jit(solution)/shard_map/stack | solution.py:33
  61.4 3.7 %all-to-all-start.2 = ((bf16[16,2,16,1024]{3,2,1,0:T(8,128)(2,1)}), bf16[16,2,16,1024]{3,2,1,0:T(8,128)(2,1)S(1)}, u32[]{:S(2)}, u32[]{:S(2)}) async-start(bf16[16,2,16,1024]{3,2,1,0:T(8,128)(2,1)} %copy.15), calls=%async_computation.2 | async-start | bytes 2097152 | tf_op jit(solution)/shard_map/all_to_all | solution.py:34
  65.1 28.9 %all-to-all-done.2 = bf16[16,2,16,1024]{3,2,1,0:T(8,128)(2,1)S(1)} async-done(((bf16[16,2,16,1024]{3,2,1,0:T(8,128)(2,1)}), bf16[16,2,16,1024]{3,2,1,0:T(8,128)(2,1)S(1)}, u32[]{:S(2)}, u32[]{:S(2)}) %all-to-all-start.2) | async-done | bytes 1048608 | tf_op jit(solution)/shard_map/all_to_all | solution.py:34
  94.1 0.1 fusion.12
  94.1 0.1 fusion.11
  94.2 0.1 maximum_bitcast_fusion
  94.3 0.6 copy.20
  94.9 1.6 %copy.23 = bf16[4,8,16,1024]{3,1,2,0:T(8,128)(2,1)} copy(bf16[4,8,16,1024]{3,2,1,0:T(8,128)(2,1)S(1)} %bitcast.50) | data formatting | bytes 2097152
  (2 shorter events, 0.1 us)
Async XLA Ops:
  31.3 21.5 %copy-start = (f32[512]{0:T(512)S(1)}, f32[512]{0:T(512)}, u32[]{:S(2)}) copy-start(f32[512]{0:T(512)} %param.6) | copy-start | bytes 6148
  47.0 10.7 %collective-permute-start = (bf16[256,1792]{1,0:T(8,128)(2,1)S(1)}, bf16[256,1792]{1,0:T(8,128)(2,1)}, u32[]{:S(2)}, u32[]{:S(2)}) collective-permute-start(bf16[256,1792]{1,0:T(8,128)(2,1)S(1)} %bitcast.53), channel_id=1, source_target_pairs={{0,16},{16,0},{1,17},{17,1},{2,18},{18,2},{3,19},{19,3},{4,20},{20... | collective-permute-start | bytes 2752520 | tf_op jit(solution)/shard_map/ppermute | solution.py:20
  54.3 3.4 %copy-start.1 = (bf16[1792,1024]{1,0:T(8,128)(2,1)S(1)}, bf16[1792,1024]{1,0:T(8,128)(2,1)}, u32[]{:S(2)}) copy-start(bf16[1792,1024]{1,0:T(8,128)(2,1)} %param.5) | copy-start | bytes 11010052
  61.4 32.7 %all-to-all-start.2 = ((bf16[16,2,16,1024]{3,2,1,0:T(8,128)(2,1)}), bf16[16,2,16,1024]{3,2,1,0:T(8,128)(2,1)S(1)}, u32[]{:S(2)}, u32[]{:S(2)}) async-start(bf16[16,2,16,1024]{3,2,1,0:T(8,128)(2,1)} %copy.15), calls=%async_computation.2 | async-start | bytes 2097152 | tf_op jit(solution)/shard_map/all_to_all | solution.py:34

commit v2 on v1

v2 whole, which is shorter than its diff:
```python
import functools

import jax
import jax.numpy as jnp
from jax import lax
from jax.experimental import pallas as pl
from jax.experimental.pallas import tpu as pltpu
from jax.sharding import Mesh, PartitionSpec as P

FINE = ("z", "yl", "c", "yh", "x")
SIZES = (8, 2, 2, 4, 4)
TILE = 256


def spread(value, axes, peers):
    copies = jnp.broadcast_to(value[None], (peers,) + value.shape)
    return lax.all_to_all(copies, axes, split_axis=0, concat_axis=0, tiled=True)


def update_kernel(where, rows_ref, integrals_ref, virt_ref, occ_ref, *rest):
    out_ref = rest[-1]
    slot = where[0]
    occ = occ_ref[pl.ds(slot * 256, 256), :]

    @pl.loop(0, 1024 // TILE)
    def _(tile):
        columns = pl.ds(pl.multiple_of(tile * TILE, TILE), TILE)
        ladder = jnp.dot(
            rows_ref[...], integrals_ref[:, columns], preferred_element_type=jnp.float32
        )
        gap = virt_ref[:, columns] - occ
        result = (ladder / gap).astype(jnp.bfloat16)
        out_ref[:, pl.ds(slot, 1), :, columns] = result.reshape(16, 1, 16, TILE)


def update(slot, rows, integrals, virt, occ, into=None):
    vmem = pl.BlockSpec(memory_space=pltpu.VMEM)
    operands = [jnp.reshape(slot, (1,)), rows, integrals, virt, occ]
    specs = [pl.BlockSpec(memory_space=pltpu.SMEM)] + [vmem] * 4
    aliases = {}
    if into is not None:
        aliases = {len(operands): 0}
        operands.append(into)
        specs.append(pl.BlockSpec(memory_space=pl.ANY))
    return pl.pallas_call(
        update_kernel,
        in_specs=specs,
        out_specs=vmem,
        out_shape=jax.ShapeDtypeStruct((16, 2, 16, 1024), jnp.bfloat16),
        input_output_aliases=aliases,
        compiler_params=pltpu.CompilerParams(vmem_limit_bytes=24 << 20),
        cost_estimate=pl.CostEstimate(
            flops=2 * 256 * 1792 * 1024, bytes_accessed=5 << 20, transcendentals=0
        ),
    )(*operands)


def place_kernel(got_ref, out_ref, sems):
    copies = [
        pltpu.make_async_copy(
            got_ref.at[source], out_ref.at[:, pl.ds(source * 1024, 1024)], sems.at[source]
        )
        for source in range(16)
    ]
    for copy in copies:
        copy.start()
    for copy in copies:
        copy.wait()


def place(got):
    return pl.pallas_call(
        place_kernel,
        in_specs=[pl.BlockSpec(memory_space=pltpu.VMEM)],
        out_specs=pl.BlockSpec(memory_space=pl.ANY),
        out_shape=jax.ShapeDtypeStruct((32, 16384), jnp.bfloat16),
        scratch_shapes=[pltpu.SemaphoreType.DMA((16,))],
    )(got)


def shards(amplitudes, integrals, occ_energy, virt_energy):
    core = lax.axis_index("c")
    member = lax.axis_index(("yh", "x"))
    virt = lax.dynamic_slice_in_dim(virt_energy, member * 1024, 1024, 0)[None]
    occ = occ_energy.reshape(16, 2, 16).transpose(1, 0, 2).reshape(512, 1)
    occ = jnp.broadcast_to(occ, (512, TILE))

    row = amplitudes.reshape(14, 128)
    plane = spread(row, ("z", "yl", "yh"), 64)
    half = spread(plane, ("x",), 4)
    half = half.reshape(4, 16, 4, 14, 128).transpose(1, 2, 0, 3, 4).reshape(256, 1792)
    other = lax.ppermute(half, "c", [(0, 1), (1, 0)])

    out = update(core, half, integrals, virt, occ)
    out = update(1 - core, other, integrals, virt, occ, out)
    got = lax.all_to_all(
        out.reshape(16, 32, 1024), ("yh", "x"), split_axis=0, concat_axis=0, tiled=True
    )
    return place(got)


def solution(mesh):
    fine = Mesh(mesh.devices.reshape(SIZES), FINE)
    return jax.shard_map(
        shards,
        mesh=fine,
        in_specs=(
            P(FINE, None),
            P(None, FINE),
            P(),
            P(("z", "yl", "c")),
        ),
        out_specs=P(("yh", "x"), ("z", "yl", "c")),
        check_vma=False,
    )
```

time: 96.8 us -> 94.4 us (0.975)
  blocking collectives: 45 us -> 77 us
  waiting for transfers between devices: 28.9 us -> 0.01 us
  Pallas kernels: 0 us -> 5.82 us
  matrix products: 5.67 us -> 0 us
  starting transfers between devices: 9.57 us -> 5.85 us
  local copies, waits for them, and re-layouts: 5.81 us -> 4.44 us
    all_to_all x0 -> x1, blocking collectives: none -> 32 us  [shards(): lax.all_to_all(out.reshape(16, 32, 1024), ('yh', 'x'), split_axis=0, conc...]
    all_to_all x1 -> x0, waiting for transfers between devices: 28.9 us -> none  [shards(): lax.all_to_all(pair, ('yh', 'x'), split_axis=0, concat_axis=0, tiled=True)]
    pallas_call x0 -> x3, Pallas kernels: none -> 5.82 us  [the longest x2 3.51 us: update(): pl.pallas_call(update_kernel, in_specs=specs, out_specs=vmem, out_shape=j...]
    dot_general x2 -> x0, matrix products: 5.67 us -> none  [update(): ladder = jnp.dot(rows, integrals, preferred_element_type=jnp.float32)]
    all_to_all x1 -> x0, starting transfers between devices: 3.72 us -> none  [shards(): lax.all_to_all(pair, ('yh', 'x'), split_axis=0, concat_axis=0, tiled=True)]
    another operation x1 -> x0, local copies, waits for them, and re-layouts: 1.05 us -> none  [shards(): pair = jnp.stack([update(half, core), update(other, 1 - core)], axis=1)]
    unnamed x6 -> x7, local copies, waits for them, and re-layouts: 1.81 us -> 2.53 us
  transfers between devices with their start and end apart: 2 -> 1, of which waited for: 1 -> 0; matrix products, arithmetic and copies ran while one was open for 5% -> 1% of each run, Pallas kernels for 0% -> 2%
where the time goes in v2:
time: 94.4 us; the launch traced here: 94 us
  blocking collectives  77 us (82%)
  starting transfers between devices  5.85 us (6%)
  Pallas kernels  5.82 us (6%)
  local copies, waits for them, and re-layouts  4.44 us (5%)
    all_to_all x2, blocking collectives, spread(): return lax.all_to_all(copies, axes, split_axis=0, concat_axis=0, tiled=True)  45 us
    all_to_all x1, blocking collectives, shards(): lax.all_to_all(out.reshape(16, 32, 1024), ('yh', 'x'), split_axis=0, conc...  32 us
    ppermute x1, starting transfers between devices, shards(): other = lax.ppermute(half, 'c', [(0, 1), (1, 0)])  5.85 us
    pallas_call x2, Pallas kernels, update(): pl.pallas_call(update_kernel, in_specs=specs, out_specs=vmem, out_shape=j...  3.51 us
    unnamed x7, local copies, waits for them, and re-layouts  2.53 us
    pallas_call x1, Pallas kernels, place(): pl.pallas_call(place_kernel, in_specs=[pl.BlockSpec(memory_space=pltpu.VM...  2.31 us
  transfers between devices with their start and end apart: 1, of which 0 were waited for; matrix products, arithmetic and copies ran while one was open for 1% of the time, Pallas kernels for 2%

profile of v2, /device:TPU:1, one launch (start us, length us, event | category | flops | bytes accessed | tf_op | source)
XLA Modules:
  0.0 94.0 jit_solution(9512523030977226627)
XLA Ops:
  0.0 0.7 reduce
  0.8 30.5 %all_to_all.15 = bf16[64,14,128]{2,1,0:T(8,128)(2,1)S(1)} all-to-all(bf16[64,14,128]{2,1,0:T(8,128)(2,1)S(1)} %broadcast_in_dim.24), channel_id=1, replica_groups=mesh['z'=8,'yl'=2,'c'=2,'yh'=4,'x'=4] {'z','yl','yh'}, dimensions={0} | all-to-all | bytes 458752 | tf_op jit(solution)/shard_map/all_to_all | solution.py:17
  31.3 0.0 copy-start.2
  31.3 0.1 copy.9
  31.4 0.2 broadcast_in_dim.25
  31.6 14.5 %all_to_all.16 = bf16[4,64,14,128]{3,1,2,0:T(8,128)(2,1)S(1)} all-to-all(bf16[4,64,14,128]{3,1,2,0:T(8,128)(2,1)S(1)} %broadcast_in_dim.25), channel_id=1, replica_groups=mesh['z'=8,'yl'=2,'c'=2,'yh'=4,'x'=4] {'x'}, dimensions={0} | all-to-all | bytes 1835008 | tf_op jit(solution)/shard_map/all_to_all | solution.py:17
  46.1 0.6 copy.10
  46.7 0.2 copy.14
  47.0 5.8 %collective-permute-start = (bf16[256,1792]{1,0:T(8,128)(2,1)S(1)}, bf16[256,1792]{1,0:T(8,128)(2,1)S(1)}, u32[]{:S(2)}, u32[]{:S(2)}) collective-permute-start(bf16[256,1792]{1,0:T(8,128)(2,1)S(1)} %bitcast.14), channel_id=1, source_target_pairs={{0,16},{16,0},{1,17},{17,1},{2,18},{18,2},{3,19},{19,3},{4,20},{20... | collective-permute-start | bytes 2752520 | tf_op jit(solution)/shard_map/ppermute | solution.py:92
  52.8 0.0 copy-done.2
  52.8 0.1 reshape.25
  52.9 0.1 broadcast_in_dim.27
  53.0 0.7 dynamic_slice.3
  53.7 0.1 broadcast_in_dim.28.occ_ref
  53.8 0.0 copy-start
  53.9 2.0 %copy-done = bf16[1792,1024]{1,0:T(8,128)(2,1)S(1)} copy-done((bf16[1792,1024]{1,0:T(8,128)(2,1)S(1)}, bf16[1792,1024]{1,0:T(8,128)(2,1)}, u32[]{:S(2)}) %copy-start) | copy-done | bytes 3670040
  55.9 0.0 copy-start.1
  55.9 1.8 %shard_map.46.rest_0_ = bf16[16,2,16,1024]{3,2,1,0:T(8,128)(2,1)S(1)} custom-call(s32[1]{0:T(128)} %bitcast.5.where, bf16[256,1792]{1,0:T(8,128)(2,1)S(1)} %bitcast.15, bf16[1792,1024]{1,0:T(8,128)(2,1)S(1)} %copy-done, f32[1,1024]{1,0:T(1,128)S(1)} %bitcast.16, f32[512,256]{1,0:T(8,128)S(1)} %broadcast_in_dim.28.occ_ref), custom_call_target="tpu_custom_call" | custom-call | flops 939524096 | bytes 5242880 | tf_op jit(solution)/shard_map/pallas_call | solution.py:45
  57.7 0.0 collective-permute-done.rows_ref
  57.7 0.3 copy-done.1
  57.9 1.7 %shard_map.47 = bf16[16,2,16,1024]{3,2,1,0:T(8,128)(2,1)S(1)} custom-call(s32[1]{0:T(128)} %bitcast.where, bf16[256,1792]{1,0:T(8,128)(2,1)S(1)} %collective-permute-done.rows_ref, bf16[1792,1024]{1,0:T(8,128)(2,1)S(1)} %copy-done.1, f32[1,1024]{1,0:T(1,128)S(1)} %bitcast.17, ...), custom_call_target="tpu_custom_call", output_to_operand_aliasing={{}: (5, {})} | custom-call | flops 939524096 | bytes 5242880 | tf_op jit(solution)/shard_map/pallas_call | solution.py:45
  59.7 32.0 %all_to_all.17.got_ref = bf16[16,32,1024]{2,1,0:T(8,128)(2,1)} all-to-all(bf16[16,32,1024]{2,1,0:T(8,128)(2,1)S(1)} %bitcast.13), channel_id=1, replica_groups=mesh['z'=8,'yl'=2,'c'=2,'yh'=4,'x'=4] {'yh','x'}, dimensions={0} | all-to-all | bytes 2097152 | tf_op jit(solution)/shard_map/all_to_all | solution.py:96
  91.7 2.3 %shard_map.48 = bf16[32,16384]{1,0:T(8,128)(2,1)} custom-call(bf16[16,32,1024]{2,1,0:T(8,128)(2,1)} %all_to_all.17.got_ref), custom_call_target="tpu_custom_call" | custom-call | tf_op jit(solution)/shard_map/pallas_call | solution.py:72
  (2 shorter events, 0.0 us)
Async XLA Ops:
  31.3 21.5 %copy-start.2 = (f32[512]{0:T(512)S(1)}, f32[512]{0:T(512)}, u32[]{:S(2)}) copy-start(f32[512]{0:T(512)} %param.6) | copy-start | bytes 6148
  47.0 10.7 %collective-permute-start = (bf16[256,1792]{1,0:T(8,128)(2,1)S(1)}, bf16[256,1792]{1,0:T(8,128)(2,1)S(1)}, u32[]{:S(2)}, u32[]{:S(2)}) collective-permute-start(bf16[256,1792]{1,0:T(8,128)(2,1)S(1)} %bitcast.14), channel_id=1, source_target_pairs={{0,16},{16,0},{1,17},{17,1},{2,18},{18,2},{3,19},{19,3},{4,20},{20... | collective-permute-start | bytes 2752520 | tf_op jit(solution)/shard_map/ppermute | solution.py:92
  53.8 2.0 %copy-start = (bf16[1792,1024]{1,0:T(8,128)(2,1)S(1)}, bf16[1792,1024]{1,0:T(8,128)(2,1)}, u32[]{:S(2)}) copy-start(bf16[1792,1024]{1,0:T(8,128)(2,1)} %integrals_ref.3) | copy-start | bytes 11010052
  55.9 2.0 %copy-start.1 = (bf16[1792,1024]{1,0:T(8,128)(2,1)S(1)}, bf16[1792,1024]{1,0:T(8,128)(2,1)}, u32[]{:S(2)}) copy-start(bf16[1792,1024]{1,0:T(8,128)(2,1)} %integrals_ref.3) | copy-start | bytes 11010052

commit v3 on v1

v3 whole, which is shorter than its diff:
```python
import jax
import jax.numpy as jnp
from jax import lax
from jax.experimental import pallas as pl
from jax.experimental.pallas import tpu as pltpu
from jax.sharding import Mesh, PartitionSpec as P

FINE = ("z", "yl", "c", "yh", "x")
SIZES = (8, 2, 2, 4, 4)
TILE = 512
TILES = 1024 // TILE
DEEP = 256
BANDS = 1792 // DEEP


def spread(value, axes, peers):
    copies = jnp.broadcast_to(value[None], (peers,) + value.shape)
    return lax.all_to_all(copies, axes, split_axis=0, concat_axis=0, tiled=True)


def divide(ladder, virt, occ, tile):
    parts = []
    for part in range(TILE // 128):
        at = tile * (TILE // 128) + part
        gap = virt[at : at + 1] - occ
        parts.append((ladder[:, part * 128 : part * 128 + 128] / gap).astype(jnp.bfloat16))
    return jnp.concatenate(parts, axis=1)


def first_kernel(
    where, rows_ref, integrals_ref, virt_ref, occ_ref, out_ref, held_ref, total, sems
):
    slot, member = where[0], where[1]
    bands = [slice(band * DEEP, (band + 1) * DEEP) for band in range(BANDS)]
    copies = [
        pltpu.make_async_copy(integrals_ref.at[rows], held_ref.at[rows], sems.at[band])
        for band, rows in enumerate(bands)
    ]
    for copy in copies:
        copy.start()
    occ = occ_ref[pl.ds(slot * 256, 256), :]
    virt = virt_ref[pl.ds(member * 8, 8), :]
    for band, rows in enumerate(bands):
        copies[band].wait()
        for tile in range(TILES):
            columns = slice(tile * TILE, (tile + 1) * TILE)
            ladder = jnp.dot(
                rows_ref[:, rows], held_ref[rows, columns], preferred_element_type=jnp.float32
            )
            if band > 0:
                ladder = ladder + total[:, columns]
            if band < BANDS - 1:
                total[:, columns] = ladder
            else:
                result = divide(ladder, virt, occ, tile)
                out_ref[:, pl.ds(slot, 1), :, columns] = result.reshape(16, 1, 16, TILE)


def second_kernel(where, rows_ref, held_ref, virt_ref, occ_ref, into_ref, out_ref):
    del into_ref
    slot, member = 1 - where[0], where[1]
    occ = occ_ref[pl.ds(slot * 256, 256), :]
    virt = virt_ref[pl.ds(member * 8, 8), :]
    for tile in range(TILES):
        columns = slice(tile * TILE, (tile + 1) * TILE)
        ladder = jnp.dot(
            rows_ref[...], held_ref[:, columns], preferred_element_type=jnp.float32
        )
        result = divide(ladder, virt, occ, tile)
        out_ref[:, pl.ds(slot, 1), :, columns] = result.reshape(16, 1, 16, TILE)


VMEM = pl.BlockSpec(memory_space=pltpu.VMEM)
SMEM = pl.BlockSpec(memory_space=pltpu.SMEM)
ANY = pl.BlockSpec(memory_space=pl.ANY)
UPDATED = jax.ShapeDtypeStruct((16, 2, 16, 1024), jnp.bfloat16)
PARAMS = pltpu.CompilerParams(vmem_limit_bytes=48 << 20)
COST = pl.CostEstimate(
    flops=2 * 256 * 1792 * 1024, bytes_accessed=5 << 20, transcendentals=0
)


def update_first(where, rows, integrals, virt, occ):
    return pl.pallas_call(
        first_kernel,
        in_specs=[SMEM, VMEM, ANY, VMEM, VMEM],
        out_specs=(VMEM, VMEM),
        out_shape=(UPDATED, jax.ShapeDtypeStruct((1792, 1024), jnp.bfloat16)),
        scratch_shapes=[pltpu.VMEM((256, 1024), jnp.float32), pltpu.SemaphoreType.DMA((BANDS,))],
        compiler_params=PARAMS,
        cost_estimate=COST,
    )(where, rows, integrals, virt, occ)


def update_second(where, rows, held, virt, occ, into):
    return pl.pallas_call(
        second_kernel,
        in_specs=[SMEM, VMEM, VMEM, VMEM, VMEM, ANY],
        out_specs=VMEM,
        out_shape=UPDATED,
        input_output_aliases={5: 0},
        compiler_params=PARAMS,
        cost_estimate=COST,
    )(where, rows, held, virt, occ, into)


def gather(amplitudes):
    row = amplitudes.reshape(14, 128)
    plane = spread(row, ("z", "yh"), 32)
    half = spread(plane, ("yl", "x"), 8).reshape(2, 4, 8, 4, 14, 128)
    return half.transpose(2, 0, 3, 1, 4, 5).reshape(256, 1792)


def shards(amplitudes, integrals, occ_energy, virt_energy):
    core = lax.axis_index("c")
    member = lax.axis_index(("yh", "x"))
    where = jnp.stack([core, member])
    virt = virt_energy.reshape(128, 128)
    occ = occ_energy.reshape(16, 2, 16).transpose(1, 0, 2).reshape(512, 1)
    occ = jnp.broadcast_to(occ, (512, 128))

    half = gather(amplitudes)
    other = lax.ppermute(half, "c", [(0, 1), (1, 0)])
    out, held = update_first(where, half, integrals, virt, occ)
    out = update_second(where, other, held, virt, occ, out)
    got = lax.all_to_all(
        out.reshape(16, 32, 1024), ("yh", "x"), split_axis=0, concat_axis=0, tiled=True
    )
    return got.transpose(1, 0, 2).reshape(32, 16384)


def solution(mesh):
    fine = Mesh(mesh.devices.reshape(SIZES), FINE)
    return jax.shard_map(
        shards,
        mesh=fine,
        in_specs=(
            P(FINE, None),
            P(None, FINE),
            P(),
            P(("z", "yl", "c")),
        ),
        out_specs=P(("yh", "x"), ("z", "yl", "c")),
        check_vma=False,
    )
```

time: 96.8 us -> 88.6 us (0.915)
  blocking collectives: 45 us -> 75 us
  waiting for transfers between devices: 28.9 us -> 0.01 us
  matrix products: 5.67 us -> 0 us
  Pallas kernels: 0 us -> 4.77 us
  starting transfers between devices: 9.57 us -> 5.45 us
  local copies, waits for them, and re-layouts: 5.81 us -> 2.18 us
    all_to_all x0 -> x1, blocking collectives: none -> 31.6 us  [shards(): lax.all_to_all(out.reshape(16, 32, 1024), ('yh', 'x'), split_axis=0, conc...]
    all_to_all x1 -> x0, waiting for transfers between devices: 28.9 us -> none  [shards(): lax.all_to_all(pair, ('yh', 'x'), split_axis=0, concat_axis=0, tiled=True)]
    dot_general x2 -> x0, matrix products: 5.67 us -> none  [update(): ladder = jnp.dot(rows, integrals, preferred_element_type=jnp.float32)]
    pallas_call x0 -> x2, Pallas kernels: none -> 4.77 us  [the longest x1 3.06 us: update_first(): pl.pallas_call(first_kernel, in_specs=[SMEM, VMEM, ANY, VMEM, VMEM], out_...]
    all_to_all x1 -> x0, starting transfers between devices: 3.72 us -> none  [shards(): lax.all_to_all(pair, ('yh', 'x'), split_axis=0, concat_axis=0, tiled=True)]
    all_to_all x2, blocking collectives: 45 us -> 43.4 us  [spread(): return lax.all_to_all(copies, axes, split_axis=0, concat_axis=0, tiled=True)]
    unnamed x6 -> x5, local copies, waits for them, and re-layouts: 1.81 us -> 0.25 us
    another operation x1 -> x0, local copies, waits for them, and re-layouts: 1.05 us -> none  [shards(): pair = jnp.stack([update(half, core), update(other, 1 - core)], axis=1)]
  transfers between devices with their start and end apart: 2 -> 1, of which waited for: 1 -> 0; matrix products, arithmetic and copies ran while one was open for 5% -> 0% of each run, Pallas kernels for 0% -> 3%
where the time goes in v3:
time: 88.6 us; the launch traced here: 88.3 us
  blocking collectives  75 us (85%)
  starting transfers between devices  5.45 us (6%)
  Pallas kernels  4.77 us (5%)
  local copies, waits for them, and re-layouts  2.18 us (2%)
    all_to_all x2, blocking collectives, spread(): return lax.all_to_all(copies, axes, split_axis=0, concat_axis=0, tiled=True)  43.4 us
    all_to_all x1, blocking collectives, shards(): lax.all_to_all(out.reshape(16, 32, 1024), ('yh', 'x'), split_axis=0, conc...  31.6 us
    ppermute x1, starting transfers between devices, shards(): other = lax.ppermute(half, 'c', [(0, 1), (1, 0)])  5.45 us
    pallas_call x1, Pallas kernels, update_first(): pl.pallas_call(first_kernel, in_specs=[SMEM, VMEM, ANY, VMEM, VMEM], out_...  3.06 us
  transfers between devices with their start and end apart: 1, of which 0 were waited for; matrix products, arithmetic and copies ran while one was open for 0% of the time, Pallas kernels for 3%

profile of v3, /device:TPU:1, one launch (start us, length us, event | category | flops | bytes accessed | tf_op | source)
XLA Modules:
  0.0 88.3 jit_solution(2318575540361564026)
XLA Ops:
  0.0 0.7 reduce
  0.7 0.0 copy-start.1
  0.8 27.6 %all_to_all.15 = bf16[32,14,128]{2,1,0:T(8,128)(2,1)S(1)} all-to-all(bf16[32,14,128]{2,1,0:T(8,128)(2,1)S(1)} %broadcast_in_dim.21), channel_id=1, replica_groups=mesh['z'=8,'yl'=2,'c'=2,'yh'=4,'x'=4] {'z','yh'}, dimensions={0} | all-to-all | bytes 229376 | tf_op jit(solution)/shard_map/all_to_all | solution.py:18
  28.4 0.0 copy-start
  28.4 0.1 broadcast_in_dim.22
  28.6 15.7 %all_to_all.16 = bf16[8,32,14,128]{3,1,2,0:T(8,128)(2,1)S(1)} all-to-all(bf16[8,32,14,128]{3,1,2,0:T(8,128)(2,1)S(1)} %broadcast_in_dim.22), channel_id=1, replica_groups=mesh['z'=8,'yl'=2,'c'=2,'yh'=4,'x'=4] {'yl','x'}, dimensions={0} | all-to-all | bytes 1835008 | tf_op jit(solution)/shard_map/all_to_all | solution.py:18
  44.3 0.4 copy.13
  44.7 0.2 copy.19
  44.9 5.5 %collective-permute-start = (bf16[256,1792]{1,0:T(8,128)(2,1)S(1)}, bf16[256,1792]{1,0:T(8,128)(2,1)S(1)}, u32[]{:S(2)}, u32[]{:S(2)}) collective-permute-start(bf16[256,1792]{1,0:T(8,128)(2,1)S(1)} %bitcast.18), channel_id=1, source_target_pairs={{0,16},{16,0},{1,17},{17,1},{2,18},{18,2},{3,19},{19,3},{4,20},{20... | collective-permute-start | bytes 2752520 | tf_op jit(solution)/shard_map/ppermute | solution.py:123
  50.4 0.0 copy-done.1
  50.4 0.1 reshape.25
  50.5 0.1 broadcast_in_dim.23
  50.6 0.1 pad_add_fusion.where
  50.7 0.1 broadcast_in_dim.24.occ_ref
  50.8 0.0 copy-done
  50.8 3.1 %shard_map.46 = (bf16[16,2,16,1024]{3,2,1,0:T(8,128)(2,1)S(1)}, bf16[1792,1024]{1,0:T(8,128)(2,1)S(1)}) custom-call(s32[2]{0:T(128)S(1)} %pad_add_fusion.where, bf16[256,1792]{1,0:T(8,128)(2,1)S(1)} %bitcast.19, bf16[1792,1024]{1,0:T(8,128)(2,1)} %integrals_ref.1, f32[128,128]{1,0:T(8,128)S(1)} %bitcast.20, f32[512,128]{1,0:T(8,128)S(1)} %broadcast_in_dim.24.occ_ref), custom_call_target="tpu_custom_call" | custom-call | flops 939524096 | bytes 5242880 | tf_op jit(solution)/shard_map/pallas_call | solution.py:84
  53.9 0.0 collective-permute-done.rows_ref
  53.9 1.7 %shard_map.47 = bf16[16,2,16,1024]{3,2,1,0:T(8,128)(2,1)S(1)} custom-call(s32[2]{0:T(128)S(1)} %pad_add_fusion.where, bf16[256,1792]{1,0:T(8,128)(2,1)S(1)} %collective-permute-done.rows_ref, bf16[1792,1024]{1,0:T(8,128)(2,1)S(1)} %get-tuple-element.7.held_ref, f32[128,128]{1,0:T(8,128)S(1)} %bitcast.21, ...), custom_call_target="tpu_custom_call", output_to_operand_aliasing={{}: (5, {})} | custom-call | flops 939524096 | bytes 5242880 | tf_op jit(solution)/shard_map/pallas_call | solution.py:96
  55.6 31.6 %all_to_all.17 = bf16[16,32,1024]{2,1,0:T(8,128)(2,1)S(1)} all-to-all(bf16[16,32,1024]{2,1,0:T(8,128)(2,1)S(1)} %bitcast.17), channel_id=1, replica_groups=mesh['z'=8,'yl'=2,'c'=2,'yh'=4,'x'=4] {'yh','x'}, dimensions={0} | all-to-all | bytes 2097152 | tf_op jit(solution)/shard_map/all_to_all | solution.py:126
  87.2 1.1 %copy.16 = bf16[16,4,8,1024]{3,2,0,1:T(8,128)(2,1)} copy(bf16[16,4,8,1024]{3,2,1,0:T(8,128)(2,1)S(1)} %bitcast.22) | data formatting | bytes 2097152 | tf_op jit(solution)/shard_map/reshape | solution.py:129
  (3 shorter events, 0.1 us)
Async XLA Ops:
  0.7 49.7 %copy-start.1 = (f32[512]{0:T(512)S(1)}, f32[512]{0:T(512)}, u32[]{:S(2)}) copy-start(f32[512]{0:T(512)} %param.6) | copy-start | bytes 6148
  28.4 22.4 %copy-start = (f32[16384]{0:T(1024)S(1)}, f32[16384]{0:T(1024)}, u32[]{:S(2)}) copy-start(f32[16384]{0:T(1024)} %param.7) | copy-start | bytes 196612
  44.9 8.9 %collective-permute-start = (bf16[256,1792]{1,0:T(8,128)(2,1)S(1)}, bf16[256,1792]{1,0:T(8,128)(2,1)S(1)}, u32[]{:S(2)}, u32[]{:S(2)}) collective-permute-start(bf16[256,1792]{1,0:T(8,128)(2,1)S(1)} %bitcast.18), channel_id=1, source_target_pairs={{0,16},{16,0},{1,17},{17,1},{2,18},{18,2},{3,19},{19,3},{4,20},{20... | collective-permute-start | bytes 2752520 | tf_op jit(solution)/shard_map/ppermute | solution.py:123

commit v4 on v3

v4 whole, which is shorter than its diff:
```python
import jax
import jax.numpy as jnp
from jax import lax
from jax.experimental import pallas as pl
from jax.experimental.pallas import tpu as pltpu
from jax.sharding import Mesh, PartitionSpec as P

FINE = ("z", "yl", "c", "yh", "x")
SIZES = (8, 2, 2, 4, 4)
DEEP = 256
BANDS = 1792 // DEEP


def spread(value, axes, peers):
    copies = jnp.broadcast_to(value[None], (peers,) + value.shape)
    return lax.all_to_all(copies, axes, split_axis=0, concat_axis=0, tiled=True)


def energies(slot, member, virt_ref, occ_ref, inverse_ref):
    occ = occ_ref[:, pl.ds(slot, 1)].reshape(256, 128)
    virt = virt_ref[pl.ds(member * 8, 8), :]
    for part in range(8):
        inverse_ref[:, part * 128 : (part + 1) * 128] = 1.0 / (virt[part : part + 1] - occ)


def first_kernel(
    core_ref,
    member_ref,
    rows_ref,
    integrals_ref,
    virt_ref,
    occ_ref,
    out_ref,
    held_ref,
    other_ref,
    own_ref,
    lines_ref,
    total,
    sems,
):
    slot, member = core_ref[0], member_ref[0]
    bands = [slice(band * DEEP, (band + 1) * DEEP) for band in range(BANDS)]
    copies = [
        pltpu.make_async_copy(integrals_ref.at[rows], held_ref.at[rows], sems.at[band])
        for band, rows in enumerate(bands)
    ]
    for copy in copies:
        copy.start()
    for block in range(4):
        lines = jnp.broadcast_to(occ_ref[block : block + 1, :], (128, 128)).T
        lines_ref[block * 4 : block * 4 + 4] = lines.reshape(4, 2, 16, 128)
    energies(slot, member, virt_ref, lines_ref, own_ref)
    energies(1 - slot, member, virt_ref, lines_ref, other_ref)
    for band, rows in enumerate(bands):
        copies[band].wait()
        ladder = jnp.dot(
            rows_ref[:, rows], held_ref[rows, :], preferred_element_type=jnp.float32
        )
        if band > 0:
            ladder = ladder + total[...]
        if band < BANDS - 1:
            total[...] = ladder
        else:
            result = (ladder * own_ref[...]).astype(jnp.bfloat16)
            out_ref[:, pl.ds(slot, 1)] = result.reshape(16, 1, 16, 1024)


def second_kernel(core_ref, rows_ref, held_ref, inverse_ref, into_ref, out_ref):
    del into_ref
    slot = 1 - core_ref[0]
    ladder = jnp.dot(rows_ref[...], held_ref[...], preferred_element_type=jnp.float32)
    result = (ladder * inverse_ref[...]).astype(jnp.bfloat16)
    out_ref[:, pl.ds(slot, 1)] = result.reshape(16, 1, 16, 1024)


VMEM = pl.BlockSpec(memory_space=pltpu.VMEM)
SMEM = pl.BlockSpec(memory_space=pltpu.SMEM)
ANY = pl.BlockSpec(memory_space=pl.ANY)
UPDATED = jax.ShapeDtypeStruct((16, 2, 16, 1024), jnp.bfloat16)
PARAMS = pltpu.CompilerParams(vmem_limit_bytes=45 << 20)
COST = pl.CostEstimate(
    flops=2 * 256 * 1792 * 1024, bytes_accessed=5 << 20, transcendentals=0
)


def update_first(core, member, rows, integrals, virt, occ):
    denominators = jax.ShapeDtypeStruct((256, 1024), jnp.float32)
    return pl.pallas_call(
        first_kernel,
        in_specs=[SMEM, SMEM, VMEM, ANY, VMEM, VMEM],
        out_specs=(VMEM, VMEM, VMEM),
        out_shape=(UPDATED, jax.ShapeDtypeStruct((1792, 1024), jnp.bfloat16), denominators),
        scratch_shapes=[
            pltpu.VMEM((256, 1024), jnp.float32),
            pltpu.VMEM((16, 2, 16, 128), jnp.float32),
            pltpu.VMEM((256, 1024), jnp.float32),
            pltpu.SemaphoreType.DMA((BANDS,)),
        ],
        compiler_params=PARAMS,
        cost_estimate=COST,
    )(core, member, rows, integrals, virt, occ)


def update_second(core, rows, held, inverse, into):
    return pl.pallas_call(
        second_kernel,
        in_specs=[SMEM, VMEM, VMEM, VMEM, ANY],
        out_specs=VMEM,
        out_shape=UPDATED,
        input_output_aliases={4: 0},
        compiler_params=PARAMS,
        cost_estimate=COST,
    )(core, rows, held, inverse, into)


def gather(amplitudes):
    row = amplitudes.reshape(14, 128)
    plane = spread(row, ("z", "yh"), 32)
    half = spread(plane, ("yl", "x"), 8).reshape(2, 4, 8, 4, 14, 128)
    return half.transpose(2, 0, 3, 1, 4, 5).reshape(256, 1792)


def shards(amplitudes, integrals, occ_energy, virt_energy):
    core = lax.axis_index("c").reshape(1)
    member = lax.axis_index(("yh", "x")).reshape(1)
    virt = virt_energy.reshape(128, 128)
    occ = occ_energy.reshape(4, 128)

    half = gather(amplitudes)
    other = lax.ppermute(half, "c", [(0, 1), (1, 0)])
    out, held, inverse = update_first(core, member, half, integrals, virt, occ)
    out = update_second(core, other, held, inverse, out)
    got = lax.all_to_all(
        out.reshape(16, 32, 1024), ("yh", "x"), split_axis=0, concat_axis=0, tiled=True
    )
    return got.transpose(1, 0, 2).reshape(32, 16384)


def solution(mesh):
    fine = Mesh(mesh.devices.reshape(SIZES), FINE)
    return jax.shard_map(
        shards,
        mesh=fine,
        in_specs=(
            P(FINE, None),
            P(None, FINE),
            P(),
            P(("z", "yl", "c")),
        ),
        out_specs=P(("yh", "x"), ("z", "yl", "c")),
        check_vma=False,
    )
```

time: 88.6 us -> 87.5 us (0.988)
  Pallas kernels: 4.77 us -> 3.8 us
    pallas_call x2, Pallas kernels: 4.77 us -> 3.8 us  [the longest x1 2.66 us: update_first(): pl.pallas_call(first_kernel, in_specs=[SMEM, SMEM, VMEM, ANY, VMEM, VMEM]...]
where the time goes in v4:
time: 87.5 us; the launch traced here: 87.2 us
  blocking collectives  75.2 us (86%)
  starting transfers between devices  5.45 us (6%)
  Pallas kernels  3.8 us (4%)
  local copies, waits for them, and re-layouts  1.89 us (2%)
    all_to_all x2, blocking collectives, spread(): return lax.all_to_all(copies, axes, split_axis=0, concat_axis=0, tiled=True)  43.5 us
    all_to_all x1, blocking collectives, shards(): lax.all_to_all(out.reshape(16, 32, 1024), ('yh', 'x'), split_axis=0, conc...  31.7 us
    ppermute x1, starting transfers between devices, shards(): other = lax.ppermute(half, 'c', [(0, 1), (1, 0)])  5.45 us
    pallas_call x1, Pallas kernels, update_first(): pl.pallas_call(first_kernel, in_specs=[SMEM, SMEM, VMEM, ANY, VMEM, VMEM]...  2.66 us
  transfers between devices with their start and end apart: 1, of which 0 were waited for; matrix products, arithmetic and copies ran while one was open for 0% of the time, Pallas kernels for 3%

profile of v4, /device:TPU:1, one launch (start us, length us, event | category | flops | bytes accessed | tf_op | source)
XLA Modules:
  0.0 87.2 jit_solution(7596510267211129856)
XLA Ops:
  0.0 0.7 reduce
  0.7 0.0 copy-start
  0.8 0.0 copy-start.1
  0.8 27.8 %all_to_all.15 = bf16[32,14,128]{2,1,0:T(8,128)(2,1)S(1)} all-to-all(bf16[32,14,128]{2,1,0:T(8,128)(2,1)S(1)} %broadcast_in_dim.14), channel_id=1, replica_groups=mesh['z'=8,'yl'=2,'c'=2,'yh'=4,'x'=4] {'z','yh'}, dimensions={0} | all-to-all | bytes 229376 | tf_op jit(solution)/shard_map/all_to_all | solution.py:16
  28.6 0.1 broadcast_in_dim.15
  28.7 15.7 %all_to_all.16 = bf16[8,32,14,128]{3,1,2,0:T(8,128)(2,1)S(1)} all-to-all(bf16[8,32,14,128]{3,1,2,0:T(8,128)(2,1)S(1)} %broadcast_in_dim.15), channel_id=1, replica_groups=mesh['z'=8,'yl'=2,'c'=2,'yh'=4,'x'=4] {'yl','x'}, dimensions={0} | all-to-all | bytes 1835008 | tf_op jit(solution)/shard_map/all_to_all | solution.py:16
  44.5 0.4 copy.10
  44.8 0.2 copy.15
  45.1 5.5 %collective-permute-start = (bf16[256,1792]{1,0:T(8,128)(2,1)S(1)}, bf16[256,1792]{1,0:T(8,128)(2,1)S(1)}, u32[]{:S(2)}, u32[]{:S(2)}) collective-permute-start(bf16[256,1792]{1,0:T(8,128)(2,1)S(1)} %bitcast.18), channel_id=1, source_target_pairs={{0,16},{16,0},{1,17},{17,1},{2,18},{18,2},{3,19},{19,3},{4,20},{20... | collective-permute-start | bytes 2752520 | tf_op jit(solution)/shard_map/ppermute | solution.py:130
  50.6 0.0 copy-done
  50.6 0.0 copy-done.1
  50.6 2.7 %shard_map.46 = (bf16[16,2,16,1024]{3,2,1,0:T(8,128)(2,1)S(1)}, bf16[1792,1024]{1,0:T(8,128)(2,1)S(1)}, f32[256,1024]{1,0:T(8,128)S(1)}) custom-call(s32[1]{0:T(128)} %bitcast.core_ref, s32[1]{0:T(128)} %bitcast.3.member_ref, bf16[256,1792]{1,0:T(8,128)(2,1)S(1)} %bitcast.19, bf16[1792,1024]{1,0:T(8,128)(2,1)} %integrals_ref.1, f32[128,128]{1,0:T(8,128)S(1)} %bitcast.20, ...), custom_call_target="tpu_custom_call" | custom-call | flops 939524096 | bytes 5242880 | tf_op jit(solution)/shard_map/pallas_call | solution.py:88
  53.2 0.0 collective-permute-done.rows_ref
  53.2 1.1 %shard_map.47 = bf16[16,2,16,1024]{3,2,1,0:T(8,128)(2,1)S(1)} custom-call(s32[1]{0:T(128)} %bitcast.core_ref, bf16[256,1792]{1,0:T(8,128)(2,1)S(1)} %collective-permute-done.rows_ref, bf16[1792,1024]{1,0:T(8,128)(2,1)S(1)} %get-tuple-element.8.held_ref, f32[256,1024]{1,0:T(8,128)S(1)} %get-tuple-element.9.inverse_ref, ...), custom_call_target="tpu_custom_call", output_to_operand_aliasing={{}: (4, {})} | custom-call | flops 939524096 | bytes 5242880 | tf_op jit(solution)/shard_map/pallas_call | solution.py:105
  54.4 31.7 %all_to_all.17 = bf16[16,32,1024]{2,1,0:T(8,128)(2,1)S(1)} all-to-all(bf16[16,32,1024]{2,1,0:T(8,128)(2,1)S(1)} %bitcast.17), channel_id=1, replica_groups=mesh['z'=8,'yl'=2,'c'=2,'yh'=4,'x'=4] {'yh','x'}, dimensions={0} | all-to-all | bytes 2097152 | tf_op jit(solution)/shard_map/all_to_all | solution.py:133
  86.1 1.1 %copy.12 = bf16[16,4,8,1024]{3,2,0,1:T(8,128)(2,1)} copy(bf16[16,4,8,1024]{3,2,1,0:T(8,128)(2,1)S(1)} %bitcast.22) | data formatting | bytes 2097152 | tf_op jit(solution)/shard_map/reshape | solution.py:136
  (2 shorter events, 0.1 us)
Async XLA Ops:
  0.7 49.8 %copy-start = (f32[16384]{0:T(1024)S(1)}, f32[16384]{0:T(1024)}, u32[]{:S(2)}) copy-start(f32[16384]{0:T(1024)} %param.7) | copy-start | bytes 196612
  0.8 49.8 %copy-start.1 = (f32[512]{0:T(512)S(1)}, f32[512]{0:T(512)}, u32[]{:S(2)}) copy-start(f32[512]{0:T(512)} %param.6) | copy-start | bytes 6148
  45.1 8.2 %collective-permute-start = (bf16[256,1792]{1,0:T(8,128)(2,1)S(1)}, bf16[256,1792]{1,0:T(8,128)(2,1)S(1)}, u32[]{:S(2)}, u32[]{:S(2)}) collective-permute-start(bf16[256,1792]{1,0:T(8,128)(2,1)S(1)} %bitcast.18), channel_id=1, source_target_pairs={{0,16},{16,0},{1,17},{17,1},{2,18},{18,2},{3,19},{19,3},{4,20},{20... | collective-permute-start | bytes 2752520 | tf_op jit(solution)/shard_map/ppermute | solution.py:130

commit v5 on v4

--- a/solution.py
+++ b/solution.py
@@ -9,6 +9,7 @@
 SIZES = (8, 2, 2, 4, 4)
 DEEP = 256
 BANDS = 1792 // DEEP
+KEPT = 3
 
 
 def spread(value, axes, peers):
@@ -23,10 +24,16 @@
         inverse_ref[:, part * 128 : (part + 1) * 128] = 1.0 / (virt[part : part + 1] - occ)
 
 
+def keep_kernel(rows_ref, integrals_ref, out_ref, kept_ref):
+    del rows_ref, out_ref
+    kept_ref[...] = integrals_ref[: KEPT * DEEP]
+
+
 def first_kernel(
     core_ref,
     member_ref,
     rows_ref,
+    kept_ref,
     integrals_ref,
     virt_ref,
     occ_ref,
@@ -43,16 +50,19 @@
     copies = [
         pltpu.make_async_copy(integrals_ref.at[rows], held_ref.at[rows], sems.at[band])
         for band, rows in enumerate(bands)
+        if band >= KEPT
     ]
     for copy in copies:
         copy.start()
+    held_ref[: KEPT * DEEP] = kept_ref[...]
     for block in range(4):
         lines = jnp.broadcast_to(occ_ref[block : block + 1, :], (128, 128)).T
         lines_ref[block * 4 : block * 4 + 4] = lines.reshape(4, 2, 16, 128)
     energies(slot, member, virt_ref, lines_ref, own_ref)
     energies(1 - slot, member, virt_ref, lines_ref, other_ref)
     for band, rows in enumerate(bands):
-        copies[band].wait()
+        if band >= KEPT:
+            copies[band - KEPT].wait()
         ladder = jnp.dot(
             rows_ref[:, rows], held_ref[rows, :], preferred_element_type=jnp.float32
         )
@@ -83,11 +93,25 @@
 )
 
 
-def update_first(core, member, rows, integrals, virt, occ):
+def keep(rows, integrals):
+    return pl.pallas_call(
+        keep_kernel,
+        in_specs=[VMEM, VMEM],
+        out_specs=(VMEM, VMEM),
+        out_shape=(
+            jax.ShapeDtypeStruct(rows.shape, rows.dtype),
+            jax.ShapeDtypeStruct((KEPT * DEEP, 1024), integrals.dtype),
+        ),
+        input_output_aliases={0: 0},
+        compiler_params=pltpu.CompilerParams(vmem_limit_bytes=24 << 20),
+    )(rows, integrals)
+
+
+def update_first(core, member, rows, kept, integrals, virt, occ):
     denominators = jax.ShapeDtypeStruct((256, 1024), jnp.float32)
     return pl.pallas_call(
         first_kernel,
-        in_specs=[SMEM, SMEM, VMEM, ANY, VMEM, VMEM],
+        in_specs=[SMEM, SMEM, VMEM, VMEM, ANY, VMEM, VMEM],
         out_specs=(VMEM, VMEM, VMEM),
         out_shape=(UPDATED, jax.ShapeDtypeStruct((1792, 1024), jnp.bfloat16), denominators),
         scratch_shapes=[
@@ -98,7 +122,7 @@
         ],
         compiler_params=PARAMS,
         cost_estimate=COST,
-    )(core, member, rows, integrals, virt, occ)
+    )(core, member, rows, kept, integrals, virt, occ)
 
 
 def update_second(core, rows, held, inverse, into):
@@ -126,9 +150,9 @@
     virt = virt_energy.reshape(128, 128)
     occ = occ_energy.reshape(4, 128)
 
-    half = gather(amplitudes)
+    half, kept = keep(gather(amplitudes), integrals)
     other = lax.ppermute(half, "c", [(0, 1), (1, 0)])
-    out, held, inverse = update_first(core, member, half, integrals, virt, occ)
+    out, held, inverse = update_first(core, member, half, kept, integrals, virt, occ)
     out = update_second(core, other, held, inverse, out)
     got = lax.all_to_all(
         out.reshape(16, 32, 1024), ("yh", "x"), split_axis=0, concat_axis=0, tiled=True

time: 87.5 us -> 86.5 us (0.989)
    pallas_call x1 -> x2, Pallas kernels: 2.66 us -> 2.08 us  [the longest x1 1.98 us: update_first(): pl.pallas_call(first_kernel, in_specs=[SMEM, SMEM, VMEM, VMEM, ANY, VMEM,...]
  transfers between devices with their start and end apart: 1 -> 1, of which waited for: 0 -> 1; matrix products, arithmetic and copies ran while one was open for 0% -> 0% of each run, Pallas kernels for 3% -> 2%
where the time goes in v5:
time: 86.5 us; the launch traced here: 86.1 us
  blocking collectives  74.6 us (86%)
  starting transfers between devices  5.45 us (6%)
  Pallas kernels  3.23 us (4%)
  local copies, waits for them, and re-layouts  1.89 us (2%)
    all_to_all x2, blocking collectives, spread(): return lax.all_to_all(copies, axes, split_axis=0, concat_axis=0, tiled=True)  43.6 us
    all_to_all x1, blocking collectives, shards(): lax.all_to_all(out.reshape(16, 32, 1024), ('yh', 'x'), split_axis=0, conc...  31 us
    ppermute x1, starting transfers between devices, shards(): other = lax.ppermute(half, 'c', [(0, 1), (1, 0)])  5.45 us
    pallas_call x1, Pallas kernels, update_first(): pl.pallas_call(first_kernel, in_specs=[SMEM, SMEM, VMEM, VMEM, ANY, VMEM,...  1.98 us
  transfers between devices with their start and end apart: 1, of which 1 were waited for; matrix products, arithmetic and copies ran while one was open for 0% of the time, Pallas kernels for 2%

profile of v5, /device:TPU:1, one launch (start us, length us, event | category | flops | bytes accessed | tf_op | source)
XLA Modules:
  0.0 86.1 jit_solution(14273502263708081511)
XLA Ops:
  0.0 0.7 reduce
  0.7 0.0 copy-start
  0.8 27.9 %all_to_all.15 = bf16[32,14,128]{2,1,0:T(8,128)(2,1)S(1)} all-to-all(bf16[32,14,128]{2,1,0:T(8,128)(2,1)S(1)} %broadcast_in_dim.14), channel_id=1, replica_groups=mesh['z'=8,'yl'=2,'c'=2,'yh'=4,'x'=4] {'z','yh'}, dimensions={0} | all-to-all | bytes 229376 | tf_op jit(solution)/shard_map/all_to_all | solution.py:17
  28.7 0.1 broadcast_in_dim.15
  28.9 15.7 %all_to_all.16 = bf16[8,32,14,128]{3,1,2,0:T(8,128)(2,1)S(1)} all-to-all(bf16[8,32,14,128]{3,1,2,0:T(8,128)(2,1)S(1)} %broadcast_in_dim.15), channel_id=1, replica_groups=mesh['z'=8,'yl'=2,'c'=2,'yh'=4,'x'=4] {'yl','x'}, dimensions={0} | all-to-all | bytes 1835008 | tf_op jit(solution)/shard_map/all_to_all | solution.py:17
  44.6 0.4 copy.11
  45.0 0.0 copy-start.1
  45.0 0.0 copy-start.2
  45.0 0.2 copy.16
  45.2 0.0 copy-done
  45.2 0.1 shard_map.46
  45.4 5.5 %collective-permute-start = (bf16[256,1792]{1,0:T(8,128)(2,1)S(1)}, bf16[256,1792]{1,0:T(8,128)(2,1)S(1)}, u32[]{:S(2)}, u32[]{:S(2)}) collective-permute-start(bf16[256,1792]{1,0:T(8,128)(2,1)S(1)} %get-tuple-element.10.rows_ref), channel_id=1, source_target_pairs={{0,16},{16,0},{1,17},{17,1},{2,18},{18,2},{3,19},{19,3},{4,20},{20... | collective-permute-start | bytes 2752520 | tf_op jit(solution)/shard_map/ppermute | solution.py:154
  50.8 0.0 copy-done.1
  50.8 0.0 copy-done.2
  50.8 2.0 %shard_map.47 = (bf16[16,2,16,1024]{3,2,1,0:T(8,128)(2,1)S(1)}, bf16[1792,1024]{1,0:T(8,128)(2,1)S(1)}, f32[256,1024]{1,0:T(8,128)S(1)}) custom-call(s32[1]{0:T(128)} %bitcast.core_ref, s32[1]{0:T(128)} %bitcast.3.member_ref, bf16[256,1792]{1,0:T(8,128)(2,1)S(1)} %get-tuple-element.10.rows_ref, bf16[768,1024]{1,0:T(8,128)(2,1)S(1)} %get-tuple-element.11.kept_ref, ...), custom_call_target="tpu_custom_call" | custom-call | flops 939524096 | bytes 5242880 | tf_op jit(solution)/shard_map/pallas_call | solution.py:112
  52.8 0.1 collective-permute-done.rows_ref
  52.9 1.1 %shard_map.48 = bf16[16,2,16,1024]{3,2,1,0:T(8,128)(2,1)S(1)} custom-call(s32[1]{0:T(128)} %bitcast.core_ref, bf16[256,1792]{1,0:T(8,128)(2,1)S(1)} %collective-permute-done.rows_ref, bf16[1792,1024]{1,0:T(8,128)(2,1)S(1)} %get-tuple-element.12.held_ref, f32[256,1024]{1,0:T(8,128)S(1)} %get-tuple-element.13.inverse_ref, ...), custom_call_target="tpu_custom_call", output_to_operand_aliasing={{}: (4, {})} | custom-call | flops 939524096 | bytes 5242880 | tf_op jit(solution)/shard_map/pallas_call | solution.py:129
  54.0 31.0 %all_to_all.17 = bf16[16,32,1024]{2,1,0:T(8,128)(2,1)S(1)} all-to-all(bf16[16,32,1024]{2,1,0:T(8,128)(2,1)S(1)} %bitcast.18), channel_id=1, replica_groups=mesh['z'=8,'yl'=2,'c'=2,'yh'=4,'x'=4] {'yh','x'}, dimensions={0} | all-to-all | bytes 2097152 | tf_op jit(solution)/shard_map/all_to_all | solution.py:157
  85.1 1.1 %copy.13 = bf16[16,4,8,1024]{3,2,0,1:T(8,128)(2,1)} copy(bf16[16,4,8,1024]{3,2,1,0:T(8,128)(2,1)S(1)} %bitcast.21) | data formatting | bytes 2097152 | tf_op jit(solution)/shard_map/reshape | solution.py:160
  (2 shorter events, 0.1 us)
Async XLA Ops:
  0.7 44.5 %copy-start = (bf16[1792,1024]{1,0:T(8,128)(2,1)S(1)}, bf16[1792,1024]{1,0:T(8,128)(2,1)}, u32[]{:S(2)}) copy-start(bf16[1792,1024]{1,0:T(8,128)(2,1)} %integrals_ref.3) | copy-start | bytes 11010052
  45.0 5.9 %copy-start.1 = (f32[16384]{0:T(1024)S(1)}, f32[16384]{0:T(1024)}, u32[]{:S(2)}) copy-start(f32[16384]{0:T(1024)} %param.7) | copy-start | bytes 196612
  45.0 5.9 %copy-start.2 = (f32[512]{0:T(512)S(1)}, f32[512]{0:T(512)}, u32[]{:S(2)}) copy-start(f32[512]{0:T(512)} %param.6) | copy-start | bytes 6148
  45.4 7.5 %collective-permute-start = (bf16[256,1792]{1,0:T(8,128)(2,1)S(1)}, bf16[256,1792]{1,0:T(8,128)(2,1)S(1)}, u32[]{:S(2)}, u32[]{:S(2)}) collective-permute-start(bf16[256,1792]{1,0:T(8,128)(2,1)S(1)} %get-tuple-element.10.rows_ref), channel_id=1, source_target_pairs={{0,16},{16,0},{1,17},{17,1},{2,18},{18,2},{3,19},{19,3},{4,20},{20... | collective-permute-start | bytes 2752520 | tf_op jit(solution)/shard_map/ppermute | solution.py:154

commit v6 on v5

--- a/solution.py
+++ b/solution.py
@@ -139,9 +139,9 @@
 
 def gather(amplitudes):
     row = amplitudes.reshape(14, 128)
-    plane = spread(row, ("z", "yh"), 32)
-    half = spread(plane, ("yl", "x"), 8).reshape(2, 4, 8, 4, 14, 128)
-    return half.transpose(2, 0, 3, 1, 4, 5).reshape(256, 1792)
+    plane = spread(row, ("yh", "z"), 32)
+    half = spread(plane, ("yl", "x"), 8).reshape(2, 4, 4, 8, 14, 128)
+    return half.transpose(3, 0, 2, 1, 4, 5).reshape(256, 1792)
 
 
 def shards(amplitudes, integrals, occ_energy, virt_energy):

time: 86.5 us -> 86.4 us (level)
  no operation moved by 1% of the time
where the time goes in v6:
time: 86.4 us; the launch traced here: 86.1 us
  blocking collectives  74.5 us (86%)
  starting transfers between devices  5.57 us (6%)
  Pallas kernels  3.23 us (4%)
  local copies, waits for them, and re-layouts  1.89 us (2%)
    all_to_all x2, blocking collectives, spread(): return lax.all_to_all(copies, axes, split_axis=0, concat_axis=0, tiled=True)  43.8 us
    all_to_all x1, blocking collectives, shards(): lax.all_to_all(out.reshape(16, 32, 1024), ('yh', 'x'), split_axis=0, conc...  30.7 us
    ppermute x1, starting transfers between devices, shards(): other = lax.ppermute(half, 'c', [(0, 1), (1, 0)])  5.57 us
    pallas_call x1, Pallas kernels, update_first(): pl.pallas_call(first_kernel, in_specs=[SMEM, SMEM, VMEM, VMEM, ANY, VMEM,...  1.97 us
  transfers between devices with their start and end apart: 1, of which 1 were waited for; matrix products, arithmetic and copies ran while one was open for 0% of the time, Pallas kernels for 2%

profile of v6, /device:TPU:1, one launch (start us, length us, event | category | flops | bytes accessed | tf_op | source)
XLA Modules:
  0.0 86.1 jit_solution(2523094230879162810)
XLA Ops:
  0.0 0.7 reduce
  0.7 0.0 copy-start
  0.8 28.0 %all_to_all.15 = bf16[32,14,128]{2,1,0:T(8,128)(2,1)S(1)} all-to-all(bf16[32,14,128]{2,1,0:T(8,128)(2,1)S(1)} %broadcast_in_dim.14), channel_id=1, replica_groups=mesh['z'=8,'yl'=2,'c'=2,'yh'=4,'x'=4] {'yh','z'}, dimensions={0} | all-to-all | bytes 229376 | tf_op jit(solution)/shard_map/all_to_all | solution.py:17
  28.8 0.1 broadcast_in_dim.15
  29.0 15.8 %all_to_all.16 = bf16[8,32,14,128]{3,1,2,0:T(8,128)(2,1)S(1)} all-to-all(bf16[8,32,14,128]{3,1,2,0:T(8,128)(2,1)S(1)} %broadcast_in_dim.15), channel_id=1, replica_groups=mesh['z'=8,'yl'=2,'c'=2,'yh'=4,'x'=4] {'yl','x'}, dimensions={0} | all-to-all | bytes 1835008 | tf_op jit(solution)/shard_map/all_to_all | solution.py:17
  44.7 0.4 copy.11
  45.1 0.0 copy-start.1
  45.1 0.0 copy-start.2
  45.1 0.2 copy.16
  45.4 0.0 copy-done
  45.4 0.1 shard_map.46
  45.5 5.6 %collective-permute-start = (bf16[256,1792]{1,0:T(8,128)(2,1)S(1)}, bf16[256,1792]{1,0:T(8,128)(2,1)S(1)}, u32[]{:S(2)}, u32[]{:S(2)}) collective-permute-start(bf16[256,1792]{1,0:T(8,128)(2,1)S(1)} %get-tuple-element.10.rows_ref), channel_id=1, source_target_pairs={{0,16},{16,0},{1,17},{17,1},{2,18},{18,2},{3,19},{19,3},{4,20},{20... | collective-permute-start | bytes 2752520 | tf_op jit(solution)/shard_map/ppermute | solution.py:154
  51.1 0.0 copy-done.1
  51.1 0.0 copy-done.2
  51.1 2.0 %shard_map.47 = (bf16[16,2,16,1024]{3,2,1,0:T(8,128)(2,1)S(1)}, bf16[1792,1024]{1,0:T(8,128)(2,1)S(1)}, f32[256,1024]{1,0:T(8,128)S(1)}) custom-call(s32[1]{0:T(128)} %bitcast.core_ref, s32[1]{0:T(128)} %bitcast.3.member_ref, bf16[256,1792]{1,0:T(8,128)(2,1)S(1)} %get-tuple-element.10.rows_ref, bf16[768,1024]{1,0:T(8,128)(2,1)S(1)} %get-tuple-element.11.kept_ref, ...), custom_call_target="tpu_custom_call" | custom-call | flops 939524096 | bytes 5242880 | tf_op jit(solution)/shard_map/pallas_call | solution.py:112
  53.1 0.1 collective-permute-done.rows_ref
  53.2 1.2 %shard_map.48 = bf16[16,2,16,1024]{3,2,1,0:T(8,128)(2,1)S(1)} custom-call(s32[1]{0:T(128)} %bitcast.core_ref, bf16[256,1792]{1,0:T(8,128)(2,1)S(1)} %collective-permute-done.rows_ref, bf16[1792,1024]{1,0:T(8,128)(2,1)S(1)} %get-tuple-element.12.held_ref, f32[256,1024]{1,0:T(8,128)S(1)} %get-tuple-element.13.inverse_ref, ...), custom_call_target="tpu_custom_call", output_to_operand_aliasing={{}: (4, {})} | custom-call | flops 939524096 | bytes 5242880 | tf_op jit(solution)/shard_map/pallas_call | solution.py:129
  54.3 30.7 %all_to_all.17 = bf16[16,32,1024]{2,1,0:T(8,128)(2,1)S(1)} all-to-all(bf16[16,32,1024]{2,1,0:T(8,128)(2,1)S(1)} %bitcast.18), channel_id=1, replica_groups=mesh['z'=8,'yl'=2,'c'=2,'yh'=4,'x'=4] {'yh','x'}, dimensions={0} | all-to-all | bytes 2097152 | tf_op jit(solution)/shard_map/all_to_all | solution.py:157
  85.0 1.1 %copy.13 = bf16[16,4,8,1024]{3,2,0,1:T(8,128)(2,1)} copy(bf16[16,4,8,1024]{3,2,1,0:T(8,128)(2,1)S(1)} %bitcast.21) | data formatting | bytes 2097152 | tf_op jit(solution)/shard_map/reshape | solution.py:160
  (2 shorter events, 0.1 us)
Async XLA Ops:
  0.7 44.6 %copy-start = (bf16[1792,1024]{1,0:T(8,128)(2,1)S(1)}, bf16[1792,1024]{1,0:T(8,128)(2,1)}, u32[]{:S(2)}) copy-start(bf16[1792,1024]{1,0:T(8,128)(2,1)} %integrals_ref.3) | copy-start | bytes 11010052
  45.1 6.0 %copy-start.1 = (f32[16384]{0:T(1024)S(1)}, f32[16384]{0:T(1024)}, u32[]{:S(2)}) copy-start(f32[16384]{0:T(1024)} %param.7) | copy-start | bytes 196612
  45.1 6.0 %copy-start.2 = (f32[512]{0:T(512)S(1)}, f32[512]{0:T(512)}, u32[]{:S(2)}) copy-start(f32[512]{0:T(512)} %param.6) | copy-start | bytes 6148
  45.5 7.7 %collective-permute-start = (bf16[256,1792]{1,0:T(8,128)(2,1)S(1)}, bf16[256,1792]{1,0:T(8,128)(2,1)S(1)}, u32[]{:S(2)}, u32[]{:S(2)}) collective-permute-start(bf16[256,1792]{1,0:T(8,128)(2,1)S(1)} %get-tuple-element.10.rows_ref), channel_id=1, source_target_pairs={{0,16},{16,0},{1,17},{17,1},{2,18},{18,2},{3,19},{19,3},{4,20},{20... | collective-permute-start | bytes 2752520 | tf_op jit(solution)/shard_map/ppermute | solution.py:154
